TPU v7x, 256 devices: a whole 4x4x8 slice. The times are simulated.
256 devices in a mesh: ctx: 32 (over z, x_hi, core), head: 8 (over y, x_lo).
Axes of the slice: x: 4 (x_hi: 2, x_lo: 2; x = x_hi * 2 + x_lo), y: 4, z: 8, core: 2. Of those that a mesh axis runs over, the one named last changes fastest.
Arguments:
- queries: bfloat16 [4096, 64, 192], P('ctx', 'head'), may hold values from -8 to 8
- latent: bfloat16 [4096, 512], P('ctx'), may hold values from -6 to 6
- key_rope: bfloat16 [4096, 64], P('ctx'), may hold values from -8 to 8
- up_keys: bfloat16 [512, 64, 128], P(None, 'head'), may hold values from -0.25 to 0.25
- up_values: bfloat16 [512, 64, 128], P(None, 'head'), may hold values from -0.25 to 0.25
- out_weight: bfloat16 [8192, 7168], P('head', 'ctx'), may hold values from -1 to 1
- block_order: int32 [64], replicated, may hold values from 0 to 63, each once
Outputs:
- mixed: bfloat16 [4096, 7168], P('ctx', 'head')
Inputs may be any that keep to these rules, and one draw needn't show every extreme that they name: A permutation; row r of the prompt lies in position block block_order[r // 64].
All inputs are finite; a program needn't handle non-finite values.
Results may differ from a plain program's by a relative error of at most 0.019.
Values may be sent and summed in bfloat16 or wider, within the bound.
A program may use at most 128 MiB of HBM per device.

v0:
```python
import functools

import jax
import jax.numpy as jnp
from jax import lax
from jax.experimental import pallas as pl
from jax.experimental.pallas import tpu as pltpu
from jax.sharding import PartitionSpec as P

MESH = pl.DeviceIdType.MESH
F32 = jnp.float32
BF16 = jnp.bfloat16
NT = (((1,), (1,)), ((), ()))
LOW = -1e30


def wait(ref, sem):
    pltpu.make_async_copy(ref, ref, sem).wait()


def kernel(
    q_hbm, lat_hbm, rope_hbm, uk_hbm, uv_hbm, w_hbm, order_hbm, out_ref,
    order_ref, rope_ref, lat, keys, qp, bias, acc, top, total, q_in, uk_in, uv_in, uk, uv, w, att, part, got, summed,
    turned, final,
    in_sem, x_sem, w_sem, lz_send, lz_recv, ly_send, ly_recv, ls_send, ls_recv,
    az_send, az_recv, as_send, as_recv, c_send, c_recv, t_send, t_recv, f_send, f_recv,
):
    ctx, head = lax.axis_index("ctx"), lax.axis_index("head")
    z, xh, core = ctx // 4, (ctx // 2) % 2, ctx % 2
    y, xl = head // 2, head % 2
    factor = (192.0 ** -0.5) * 1.4426950408889634

    def at(z_, xh_, core_, y_, xl_):
        return (z_ * 4 + xh_ * 2 + core_, y_ * 2 + xl_)

    sibling = at(z, xh, 1 - core, y, xl)
    x_next = at(z, 1 - xh, core, y, 1 - xl)
    x_far = at(z, 1 - xh, core, y, xl)

    def send(src, dst, send_sem, recv_sem, device):
        pltpu.make_async_remote_copy(
            src_ref=src, dst_ref=dst, send_sem=send_sem, recv_sem=recv_sem,
            device_id=device, device_id_type=MESH,
        ).start()

    def other_head(step, core_):
        return at(z, xh, core_, (y + step // 2) % 4, (xl + step) % 2)

    barrier = pltpu.get_barrier_semaphore()
    partners = [sibling, x_next, x_far]
    partners += [at((z + step) % 8, xh, core, y, xl) for step in range(1, 8)]
    partners += [other_head(step, c) for step in range(1, 8) for c in (core, 1 - core)]
    for device in partners:
        pl.semaphore_signal(barrier, inc=1, device_id=device, device_id_type=MESH)

    my_w = w.at[pl.ds(pl.multiple_of(64 + 224 * xh, 16), 224)]
    loads = [
        pltpu.make_async_copy(src, dst, in_sem.at[i])
        for i, (src, dst) in enumerate(
            [(q_hbm, q_in), (uk_hbm, uk_in), (uv_hbm, uv_in), (w_hbm, my_w)]
            + [(lat_hbm, lat.at[z, core, xh, 0:128]), (rope_hbm, rope_ref), (order_hbm, order_ref)]
        )
    ]
    for load in loads[4:] + loads[0:4]:
        load.start()

    for load in loads[4:]:
        load.wait()
    rope = jnp.concatenate([rope_ref[...].astype(F32), jnp.zeros((64, 128), F32)], axis=0).T
    rope = rope[0:64, :] + pltpu.roll(rope[64:128, :], 64, 1)
    for g in range(4):
        lat[z, core, xh, 128:144, g * 128 : (g + 1) * 128] = rope[g * 16 : (g + 1) * 16, :].astype(BF16)

    pl.semaphore_wait(barrier, len(partners))
    mine = lat.at[z, core, xh]
    send(mine, mine, x_sem.at[0], x_sem.at[1], x_next)

    carried = (xh + y) % 2

    def ring(s, side):
        zz = (z + 8 - s) % 8 if side == 0 else (z + s) % 8
        block = lat.at[zz, core, carried]
        active = (s <= 4) if side == 0 else ((s >= 1) & (s <= 3))

        @pl.when(active & (s > 0))
        def _():
            wait(block, lz_recv.at[zz])

        @pl.when((s < 3) | ((s == 3) & (core == side)))
        def _():
            to = (z + 1) % 8 if side == 0 else (z + 7) % 8
            send(block, block, lz_send.at[0], lz_recv.at[zz], at(to, xh, core, y, xl))

        down = (s <= 3) | (core == 0) if side == 0 else (s < 0)

        @pl.when(active & (s > 0) & down)
        def _():
            send(block, block, ly_send.at[0], ly_recv.at[zz], at(z, xh, core, (y + 3) % 4, xl))

        @pl.when(active & (s > 0) & jnp.logical_not(down))
        def _():
            send(block, block, ly_send.at[0], ly_recv.at[zz], at(z, xh, core, (y + 1) % 4, xl))

        @pl.when(active)
        def _():
            send(block, block, ls_send.at[0], ls_recv.at[zz, carried], sibling)

    def across(zz):
        block = lat.at[zz, core, 1 - carried]

        @pl.when(zz != z)
        def _():
            wait(block, ly_recv.at[zz])

        send(block, block, ls_send.at[0], ls_recv.at[zz, 1 - carried], sibling)

    @pl.when(carried == xh)
    def _():
        ring(0, 0)
        ring(0, 1)

    wait(mine, x_sem.at[1])

    @pl.when(carried != xh)
    def _():
        ring(0, 0)
        ring(0, 1)

    across(z)
    loads[3].wait()
    send(my_w, my_w, w_sem.at[0], w_sem.at[1], x_far)

    w[0:64, :] = jnp.zeros((64, 1024), BF16)
    w[512:576, :] = jnp.zeros((64, 1024), BF16)

    for load in loads[0:3]:
        load.wait()
    to_row = lax.broadcasted_iota(jnp.int32, (256, 256), 0)
    from_row = lax.broadcasted_iota(jnp.int32, (256, 256), 1)
    turn_rows = jnp.where(
        from_row == (to_row & 31) * 8 + (to_row >> 5), 1.0, 0.0
    ).astype(BF16)

    def by_head(i, carry):
        rows = pl.ds(pl.multiple_of(i * 256, 256), 256)
        both = jnp.concatenate([uk_in[rows, :], uv_in[rows, :]], axis=1)
        both = jnp.dot(turn_rows, both, preferred_element_type=F32).astype(BF16)
        held = pl.ds(pl.multiple_of(i * 32, 32), 32)
        for h in range(8):
            uk[h, held, :] = both[h * 32 : h * 32 + 32, 0:128]
            uv[h, held, :] = both[h * 32 : h * 32 + 32, 128:256]
        return carry

    lax.fori_loop(0, 16, by_head, 0)

    def project(h, carry):
        rows = pl.ds(pl.multiple_of(h * 128, 128), 128)
        q = q_in[h].astype(F32)
        plain = q[0:128, :].T.astype(BF16)
        qp[rows, 0:512] = lax.dot_general(
            plain, uk[h], NT, preferred_element_type=F32
        ).astype(BF16)
        turned_rope = jnp.concatenate([q[128:192, :], jnp.zeros((64, 128), F32)], axis=0).T
        qp[rows, 512:640] = turned_rope.astype(BF16)
        return carry

    lax.fori_loop(0, 8, project, 0)
    top[...] = jnp.full_like(top, LOW)
    total[...] = jnp.zeros_like(total)
    acc[...] = jnp.zeros_like(acc)

    lane = lax.broadcasted_iota(jnp.int32, (8, 512), 1)
    row = lax.broadcasted_iota(jnp.int32, (128, 512), 0)

    def load_keys(zz, slot):
        for x in range(2):
            wait(lat.at[zz, 1 - core, x], ls_recv.at[zz, x])
        place = jnp.zeros((8, 512), jnp.int32)
        for c in range(2):
            for x in range(2):
                n = c * 2 + x
                for half in range(2):
                    block = order_ref[zz * 8 + x * 4 + c * 2 + half] * 64
                    place = jnp.where((lane >> 6) == n * 2 + half, block + (lane & 63), place)
                keys[slot, n * 128 : (n + 1) * 128, 0:512] = lat[zz, c, x, 0:128, :]
                for g in range(4):
                    pair = lat[zz, c, x, 128:144, g * 128 : (g + 1) * 128]
                    keys[slot, n * 128 + g * 16 : n * 128 + g * 16 + 16, 512:640] = pair
                    turn = pltpu.roll(pair.astype(F32), 64, 1).astype(BF16)
                    keys[slot, n * 128 + 64 + g * 16 : n * 128 + 64 + g * 16 + 16, 512:640] = turn
        own = row + jnp.where(
            row < 64, order_ref[ctx * 2] * 64, order_ref[ctx * 2 + 1] * 64 - 64
        )
        bias[slot] = jnp.where(place[0:1, :] <= own, 0.0, LOW)

    def fold(slot, first, count):
        rows = slice(first * 512, (first + count) * 512)
        s = lax.dot_general(qp[rows, :], keys[slot], NT, preferred_element_type=F32)
        s = s + jnp.concatenate([bias[slot]] * (4 * count), axis=0)
        old = top[rows, :]
        new = jnp.maximum(old, jnp.max(s, axis=1, keepdims=True))
        top[rows, :] = new
        p = jnp.exp2((s - jnp.concatenate([new] * 4, axis=1)) * factor)
        fade = jnp.exp2((old - new) * factor)
        total[rows, :] = total[rows, :] * fade + (
            (p[:, 0:128] + p[:, 128:256]) + (p[:, 256:384] + p[:, 384:512])
        )
        added = jnp.dot(p.astype(BF16), keys[slot, :, 0:512], preferred_element_type=F32)
        acc[rows, :] = acc[rows, :] * jnp.concatenate([fade] * 4, axis=1) + added

    def attend(zz):
        load_keys(zz, 0)
        fold(0, 0, 2)

    def pair(s, work):
        def one(i, c):
            work(jnp.where(i == 0, (z + 8 - s) % 8, (z + s) % 8))
            return c

        lax.fori_loop(0, jnp.where((s >= 1) & (s <= 3), 2, 1), one, 0)

    def gather_step(s, carry):
        @pl.when(s >= 2)
        def _():
            pair(s - 1, across)

        ring(s, 0)
        ring(s, 1)

        @pl.when(s <= 3)
        def _():
            pair(s - 1, attend)

        return carry

    lax.fori_loop(1, 5, gather_step, 0)

    def att_ring(s, side, u):
        zz = (z + 8 - s) % 8 if side == 0 else (z + s) % 8
        block = att.at[zz, core, u]
        active = (s >= 0) if side == 0 else ((s >= 1) & (s <= 3))

        @pl.when(active & (s > 0))
        def _():
            wait(block, az_recv.at[zz, u])

        @pl.when((s < 3) | ((s == 3) & (core == side)))
        def _():
            to = (z + 1) % 8 if side == 0 else (z + 7) % 8
            send(block, block, az_send.at[0], az_recv.at[zz, u], at(to, xh, core, y, xl))

        @pl.when(active)
        def _():
            send(block, block, as_send.at[0], as_recv.at[zz, u], sibling)

    def finish(u):
        for v in range(4):
            h = u * 4 + v
            rows = slice(h * 128, h * 128 + 128)
            scale = 1.0 / jnp.sum(total[rows, :], axis=1, keepdims=True)
            att[z, core, u, :, v * 128 : v * 128 + 128] = jnp.dot(
                (acc[rows, :] * scale).astype(BF16), uv[h], preferred_element_type=F32
            ).astype(BF16)
        att_ring(0, 0, u)
        att_ring(0, 1, u)

    load_keys((z + 5) % 8, 0)
    load_keys((z + 3) % 8, 1)
    fold(0, 0, 1)
    fold(1, 0, 1)
    across((z + 4) % 8)
    load_keys((z + 4) % 8, 2)
    fold(2, 0, 1)
    finish(0)
    for slot in range(3):
        fold(slot, 1, 1)
    finish(1)
    wait(my_w, w_sem.at[1])

    def multiply(zz):
        for u in range(2):
            wait(att.at[zz, 1 - core, u], as_recv.at[zz, u])

        def product(c, rows):
            return sum(
                lax.dot_general(
                    att[zz, c, u], w[rows, u * 512 : u * 512 + 512], NT, preferred_element_type=F32
                )
                for u in range(2)
            )

        a = product(0, slice(64, 576))
        b = product(1, slice(0, 512))
        part[zz, :, 0:384] = a[:, 0:384].astype(BF16)
        part[zz, :, 384:512] = (a[:, 384:512] + b[:, 0:128]).astype(BF16)
        part[zz, :, 512:896] = b[:, 128:512].astype(BF16)
        for step in range(1, 8):
            y_, xl_ = (y + step // 2) % 4, (xl + step) % 2
            rows = pl.ds(pl.multiple_of((y_ * 2 + xl_) * 16, 16), 16)
            send(
                part.at[zz, rows], got.at[zz, head], c_send.at[0], c_recv.at[zz],
                at(z, xh, core, y_, xl_),
            )
        rows = pl.ds(pl.multiple_of(head * 16, 16), 16)
        got[zz, head] = part[zz, rows, :]

    def reduce(zz):
        wait(got.at[zz, 0:7], c_recv.at[zz])
        whole = got[zz, 0].astype(F32)
        for h in range(1, 8):
            whole = whole + got[zz, h].astype(F32)

        @pl.when(zz == z)
        def _():
            turned[z] = whole.astype(BF16)

        @pl.when(zz != z)
        def _():
            summed[zz] = whole.astype(BF16)
            send(
                summed.at[zz], turned.at[z], t_send.at[0], t_recv.at[z],
                at(zz, xh, core, y, xl),
            )

    def deliver(zz):
        @pl.when(zz != z)
        def _():
            wait(turned.at[zz], t_recv.at[zz])

        for c in range(2):
            window = slice(384 * c, 384 * c + 512)
            own = (zz == head) & (core == c)

            @pl.when(own)
            def _():
                final[head * 2 + core] = turned[zz, :, window]

            @pl.when(jnp.logical_not(own))
            def _():
                send(
                    turned.at[zz, :, window], final.at[head * 2 + core],
                    f_send.at[0], f_recv.at[0], at(z, xh, c, zz // 2, zz % 2),
                )

    def output_step(s, carry):
        @pl.when((s >= 1) & (s <= 4))
        def _():
            for u in range(2):
                att_ring(s, 0, u)
                att_ring(s, 1, u)

        @pl.when(s <= 4)
        def _():
            pair(s, multiply)

        @pl.when((s >= 2) & (s <= 5))
        def _():
            pair(s - 2, reduce)

        @pl.when(s == 5)
        def _():
            reduce((z + 4) % 8)

        @pl.when(s >= 3)
        def _():
            pair(s - 3, deliver)

        return carry

    lax.fori_loop(0, 8, output_step, 0)

    wait(final.at[0:15], f_recv.at[0])
    for c in range(2):

        @pl.when(core == c)
        def _():
            def place(h, carry):
                rows = pl.ds(pl.multiple_of(h * 16, 16), 16)
                v0, v1 = final[h * 2].astype(F32), final[h * 2 + 1].astype(F32)
                empty = jnp.zeros((16, 512), F32)
                v0 = jnp.concatenate([v0, empty], axis=1)
                v1 = jnp.concatenate([v1, empty], axis=1)
                back = 64 * c
                column = lax.broadcasted_iota(jnp.int32, (16, 1024), 1)

                def turn(v, by):
                    return v if by % 1024 == 0 else pltpu.roll(v, by % 1024, 1)

                full = jnp.where(
                    column < 448,
                    jnp.where(column < 224, turn(v0, -back), turn(v1, 224 - back)),
                    jnp.where(column < 672, turn(v0, 224 - back), turn(v1, 448 - back)),
                )
                out_ref[rows, :] = full[:, 0:896].astype(BF16)
                return carry

            lax.fori_loop(0, 8, place, 0)

    wait(mine, x_sem.at[0])
    wait(my_w, w_sem.at[0])
    wait(lat.at[0:7, 0, 0], lz_send.at[0])
    wait(lat.at[0:7, 0, 0], ly_send.at[0])
    wait(lat.at[0:8, 0], ls_send.at[0])
    wait(att.at[0:7, 0], az_send.at[0])
    wait(att.at[0:8, 0], as_send.at[0])
    wait(part.at[0:7], c_send.at[0])
    wait(summed.at[0:7], t_send.at[0])
    wait(final.at[0:15], f_send.at[0])


def shards(queries, latent, key_rope, up_keys, up_values, out_weight, block_order):
    q = jnp.transpose(queries, (1, 2, 0))
    rope = jnp.transpose(key_rope)
    uk = up_keys.reshape(4096, 128)
    uv = up_values.reshape(4096, 128)
    w = jnp.transpose(out_weight)
    vmem = pl.BlockSpec(memory_space=pltpu.VMEM)
    hbm = pl.BlockSpec(memory_space=pl.ANY)
    dma = pltpu.SemaphoreType.DMA
    return pl.pallas_call(
        kernel,
        out_shape=jax.ShapeDtypeStruct((128, 896), BF16),
        in_specs=[hbm] * 7,
        out_specs=vmem,
        scratch_shapes=[
            pltpu.SMEM((64,), jnp.int32),
            pltpu.VMEM((64, 128), BF16),
            pltpu.VMEM((8, 2, 2, 144, 512), BF16),
            pltpu.VMEM((3, 512, 640), BF16),
            pltpu.VMEM((1024, 640), BF16),
            pltpu.VMEM((3, 128, 512), F32),
            pltpu.VMEM((1024, 512), F32),
            pltpu.VMEM((1024, 128), F32),
            pltpu.VMEM((1024, 128), F32),
            pltpu.VMEM((8, 192, 128), BF16),
            pltpu.VMEM((4096, 128), BF16),
            pltpu.VMEM((4096, 128), BF16),
            pltpu.VMEM((8, 512, 128), BF16),
            pltpu.VMEM((8, 512, 128), BF16),
            pltpu.VMEM((576, 1024), BF16),
            pltpu.VMEM((8, 2, 2, 128, 512), BF16),
            pltpu.VMEM((8, 128, 896), BF16),
            pltpu.VMEM((8, 8, 16, 896), BF16),
            pltpu.VMEM((8, 16, 896), BF16),
            pltpu.VMEM((8, 16, 896), BF16),
            pltpu.VMEM((16, 16, 512), BF16),
            dma((7,)), dma((2,)), dma((2,)),
            dma((1,)), dma((8,)), dma((1,)), dma((8,)), dma((1,)), dma((8, 2)),
            dma((1,)), dma((8, 2)), dma((1,)), dma((8, 2)),
            dma((1,)), dma((8,)),
            dma((1,)), dma((8,)),
            dma((1,)), dma((1,)),
        ],
        compiler_params=pltpu.CompilerParams(
            collective_id=0, has_side_effects=True, vmem_limit_bytes=56 * 2**20
        ),
        cost_estimate=pl.CostEstimate(
            flops=25 * 10**9, bytes_accessed=4 * 2**20, transcendentals=4 * 2**20
        ),
        name="latent_attention",
    )(q, latent, rope, uk, uv, w, block_order)


def solution(mesh):
    placed = (
        P("ctx", "head", None),
        P("ctx", None),
        P("ctx", None),
        P(None, "head", None),
        P(None, "head", None),
        P("head", "ctx"),
        P(),
    )
    return jax.shard_map(
        shards, mesh=mesh, in_specs=placed, out_specs=P("ctx", "head"), check_vma=False
    )
```

profile of v0, /device:TPU:17, one launch (start us, length us, event | category | flops | bytes accessed | tf_op | source)
XLA Modules:
  0.0 84.4 jit_solution(791983055688443761)
XLA Ops:
  0.0 82.7 %latent_attention.1 = bf16[128,896]{1,0:T(8,128)(2,1)} custom-call(bf16[8,192,128]{2,1,0:T(8,128)(2,1)} %bitcast.8, bf16[128,512]{1,0:T(8,128)(2,1)} %lat_hbm.1, bf16[64,128]{1,0:T(8,128)(2,1)} %bitcast.9, bf16[4096,128]{1,0:T(8,128)(2,1)} %bitcast.5, bf16[4096,128]{1,0:T(8,128)(2,1)} %bitcast.6, bf16[224,1024]{1,0:T(8,128)(2,1)} %bitcast.7, s32[64]{0:T(128)} %order_hbm.1), custom_call_target="tpu_custom_call" | custom-call | flops 24999999488 | bytes 4194304 | tf_op jit(solution)/shard_map/latent_attention/pallas_call | solution.py:420
  82.7 1.6 %copy.9 = bf16[128,896]{1,0:T(8,128)(2,1)} copy(bf16[128,896]{1,0:T(8,128)(2,1)} %latent_attention.1) | data formatting | bytes 458752
where the time goes:
time: 84.5 us; the launch traced here: 84.4 us
  Pallas kernels  82.7 us (98%)
  local copies, waits for them, and re-layouts  1.65 us (2%)
    pallas_call x1, Pallas kernels, shards(): pl.pallas_call(kernel, out_shape=jax.ShapeDtypeStruct((128, 896), BF16),...  82.7 us

commit v1 on v0

--- a/solution.py
+++ b/solution.py
@@ -294,7 +294,7 @@
         part[zz, :, 0:384] = a[:, 0:384].astype(BF16)
         part[zz, :, 384:512] = (a[:, 384:512] + b[:, 0:128]).astype(BF16)
         part[zz, :, 512:896] = b[:, 128:512].astype(BF16)
-        for step in range(1, 8):
+        for step in (5, 4, 3, 7, 2, 6, 1):
             y_, xl_ = (y + step // 2) % 4, (xl + step) % 2
             rows = pl.ds(pl.multiple_of((y_ * 2 + xl_) * 16, 16), 16)
             send(

time: 84.5 us -> 84.6 us (level)
  no operation moved by 1% of the time
where the time goes in v1:
time: 84.6 us; the launch traced here: 84.5 us
  Pallas kernels  82.8 us (98%)
  local copies, waits for them, and re-layouts  1.65 us (2%)
    pallas_call x1, Pallas kernels, shards(): pl.pallas_call(kernel, out_shape=jax.ShapeDtypeStruct((128, 896), BF16),...  82.8 us

profile of v1, /device:TPU:17, one launch (start us, length us, event | category | flops | bytes accessed | tf_op | source)
XLA Modules:
  0.0 84.5 jit_solution(9782802998186796521)
XLA Ops:
  0.0 82.8 %latent_attention.1 = bf16[128,896]{1,0:T(8,128)(2,1)} custom-call(bf16[8,192,128]{2,1,0:T(8,128)(2,1)} %bitcast.8, bf16[128,512]{1,0:T(8,128)(2,1)} %lat_hbm.1, bf16[64,128]{1,0:T(8,128)(2,1)} %bitcast.9, bf16[4096,128]{1,0:T(8,128)(2,1)} %bitcast.5, bf16[4096,128]{1,0:T(8,128)(2,1)} %bitcast.6, bf16[224,1024]{1,0:T(8,128)(2,1)} %bitcast.7, s32[64]{0:T(128)} %order_hbm.1), custom_call_target="tpu_custom_call" | custom-call | flops 24999999488 | bytes 4194304 | tf_op jit(solution)/shard_map/latent_attention/pallas_call | solution.py:420
  82.8 1.6 %copy.9 = bf16[128,896]{1,0:T(8,128)(2,1)} copy(bf16[128,896]{1,0:T(8,128)(2,1)} %latent_attention.1) | data formatting | bytes 458752
